TPU v7x, 128 devices: a whole 4x4x4 slice. The times are simulated.
128 devices in a mesh: group: 8 (over y, core), dev: 16 (over z, x).
Axes of the slice: x: 4, y: 4, z: 4, core: 2. Of those that a mesh axis runs over, the one named last changes fastest.
Arguments:
- embeds: bfloat16 [49152, 1024], P(('group', 'dev')), may hold values from -30 to 30, as said below
- cluster_id: int32 [49152], P(('group', 'dev')), may hold values from 0 to 23, as said below
- owner_slot: int32 [24], replicated, may hold values from 0 to 23, each once
Outputs:
- near_max: float32 [8, 16, 3, 256], P('group', 'dev')
- neighbor_logsumexp: float32 [8, 16, 3, 256], P('group', 'dev')
Inputs may be any that keep to these rules, and one draw needn't show every extreme that they name: `cluster_id`: at most 32 rows of one device name the same cluster, and every cluster is named by two or more rows. owner_slot[c] = 3 * g + l: group g owns cluster c as its l-th cluster. `embeds`: every row has a sum of squares over its 1024 features of 1 or more.
All inputs are finite; a program needn't handle non-finite values.
Results may differ from a plain program's by a relative error of at most 0.00042.
Values may be sent and summed in bfloat16 or wider, within the bound.
A program may use at most 128 MiB of HBM per device.

v0:
```python
import jax
import jax.numpy as jnp
from jax import lax
from jax.sharding import PartitionSpec as P

SOFTMAX_TEMPER = 0.05
EPSILON = 1e-06
FLOOR = -2.0
LIVE_LEVEL = -1.5


def unit_rows(embeds):
    widened = embeds.astype(jnp.float32)
    scale = lax.rsqrt(jnp.sum(widened * widened, axis=1, keepdims=True) + EPSILON)
    return (widened * scale).astype(jnp.bfloat16)


def presence(blocks):
    return jnp.sum(jnp.square(blocks.astype(jnp.float32)), axis=-1) > 0.5


def tile_scores(mine, partner):
    return jnp.einsum("csd,cpd->csp", mine, partner, preferred_element_type=jnp.float32)


def merge_stats(high_one, sum_one, high_two, sum_two):
    top = jnp.maximum(high_one, high_two)
    return (
        top,
        sum_one * jnp.exp((high_one - top) / SOFTMAX_TEMPER)
        + sum_two * jnp.exp((high_two - top) / SOFTMAX_TEMPER),
    )


def reduce_tile(similarity_scores, retained_rows, axis):
    tile_high = jnp.max(jnp.where(retained_rows, similarity_scores, FLOOR), axis=axis)
    anchor = jnp.expand_dims(tile_high, axis)
    tile_sum = jnp.sum(
        jnp.where(retained_rows, jnp.exp((similarity_scores - anchor) / SOFTMAX_TEMPER), 0.0),
        axis=axis,
    )
    return (tile_high, tile_sum)


def shards(embeds, cluster_id, owner_slot):
    rows_dev = embeds.shape[0]
    width = embeds.shape[1]
    groups = lax.axis_size("group")
    clusters = owner_slot.shape[0]
    owned = clusters // groups
    most_rows = 2 * rows_dev // clusters
    slots = groups * most_rows
    unit = unit_rows(embeds)
    onehot = (cluster_id[:, None] == jnp.arange(clusters, dtype=jnp.int32)[None, :]).astype(
        jnp.int32
    )
    ranking = jnp.sum((jnp.cumsum(onehot, axis=0) - 1) * onehot, axis=1)
    owner = jnp.sum(onehot * owner_slot[None, :], axis=1)
    position = (owner % owned * groups + owner // owned) * most_rows + ranking
    outgoing = jnp.zeros((clusters * most_rows, width), jnp.bfloat16).at[position].set(unit)
    outgoing = outgoing.reshape(owned, groups, most_rows, width)
    received = lax.all_to_all(outgoing, "group", split_axis=1, concat_axis=1, tiled=True).reshape(
        owned, slots, width
    )
    present_flags = presence(received)
    my_index = lax.axis_index("dev")
    own_index = my_index * slots + jnp.arange(slots, dtype=jnp.int32)
    piece = lax.all_gather(received, "dev", axis=1, tiled=True)
    highest = jnp.full((owned, slots), FLOOR, jnp.float32)
    summed_terms = jnp.zeros((owned, slots), jnp.float32)
    similarity_scores = tile_scores(received, piece)
    column_index = jnp.arange(piece.shape[1], dtype=jnp.int32)
    retained_rows = presence(piece)[:, None, :] & (
        column_index[None, None, :] != own_index[None, :, None]
    )
    tile_high, tile_sum = reduce_tile(similarity_scores, retained_rows, 2)
    highest, summed_terms = merge_stats(highest, summed_terms, tile_high, tile_sum)
    has_other = present_flags & (highest > LIVE_LEVEL)
    near_max = jnp.where(present_flags, highest, 0.0)
    neighbor_logsumexp = jnp.where(
        has_other, highest / SOFTMAX_TEMPER + jnp.log(jnp.where(has_other, summed_terms, 1.0)), 0.0
    )
    return (near_max[None, None], neighbor_logsumexp[None, None])


def solution(mesh):
    in_specs = (P(("group", "dev"), None), P(("group", "dev")), P())
    out_specs = (P("group", "dev", None, None), P("group", "dev", None, None))
    return jax.shard_map(shards, mesh=mesh, in_specs=in_specs, out_specs=out_specs, check_vma=False)
```

profile of v0, /device:TPU:1, one launch (start us, length us, event | category | flops | bytes accessed | tf_op | source)
XLA Modules:
  0.0 249.2 jit_solution(11238340890555488139)
XLA Ops:
  7.2 0.0 all-gather.2.cloned.1.call-start
  7.2 0.7 fusion.10
  7.9 0.9 reduce-window.6
  8.8 0.2 slice_reduce_fusion
  9.0 0.8 select_reduce_fusion
  9.8 1.4 fusion.2
  11.3 3.2 %scatter_custom_fusion = bf16[768,1024]{1,0:T(8,128)(2,1)S(1)} fusion(s32[384]{0:T(512)S(1)} %fusion.23, bf16[384,1024]{1,0:T(8,128)(2,1)} %param.3, f32[384]{0:T(512)S(1)} %add_rsqrt_fusion, bf16[]{:T(256)} %constant.20.clone.1), kind=kCustom, calls=%fused_computation.12 | custom fusion | flops 1179648 | bytes 2361346 | tf_op jit(solution)/shard_map/scatter | solution.py:60
  14.5 0.2 copy.19
  14.6 26.5 %all_to_all.5 = bf16[3,8,32,1024]{3,2,0,1:T(8,128)(2,1)S(1)} all-to-all(bf16[3,8,32,1024]{3,2,0,1:T(8,128)(2,1)S(1)} %copy.19), channel_id=1, replica_groups=mesh['group'=8,'dev'=16] {'group'}, dimensions={1} | all-to-all | bytes 3145728 | tf_op jit(solution)/shard_map/all_to_all | solution.py:62
  41.2 1.4 copy.21
  42.6 0.0 all-gather.2.cloned.1.call-update
  42.6 0.7 iota_compare_fusion
  43.3 0.4 multiply_reduce_fusion.1
  43.7 0.1 gt.45
  43.8 154.0 %all-gather.2.cloned.1.call-done = bf16[3,4096,1024]{2,1,0:T(8,128)(2,1)} async-done(((bf16[3,256,1024]{2,1,0:T(8,128)(2,1)}), bf16[3,4096,1024]{2,1,0:T(8,128)(2,1)}) %all-gather.2.cloned.1.call-update) | async-done | bytes 25165840 | tf_op jit(solution)/shard_map/all_gather | solution.py:68
  197.8 0.0 copy-start
  197.8 10.4 %multiply_reduce_fusion = f32[3,4096]{1,0:T(4,128)S(1)} fusion(bf16[3,4096,1024]{2,1,0:T(8,128)(2,1)} %all-gather.2.cloned.1.call-done), kind=kLoop, calls=%fused_computation.1 | loop fusion | flops 37736448 | bytes 25214976 | tf_op jit(solution)/shard_map/reduce_sum | solution.py:19
  208.3 0.0 copy-done
  208.3 25.9 %fusion = (f32[3,256]{1,0:T(4,128)S(1)}, f32[3,256,4096]{2,1,0:T(8,128)}) fusion(pred[256,4096]{1,0:T(8,128)(4,1)S(1)} %iota_compare_fusion, pred[3,4096]{1,0:T(4,128)(4,1)S(1)} %broadcast_compare_fusion, bf16[3,256,1024]{2,1,0:T(8,128)(2,1)S(1)} %bitcast.33, bf16[3,4096,1024]{2,1,0:T(8,128)(2,1)} %all-gather.2.cloned.1.call-done), kind=kOutput, calls=%fused_computation.4 | convolution fusion | flops 6451887104 | bytes 40385536 | tf_op jit(solution)/shard_map/csd,cpd->csp/dot_general | solution.py:23
  234.2 7.0 %fusion.1 = f32[3,256]{1,0:T(4,128)S(1)} fusion(f32[3,256,4096]{2,1,0:T(8,128)} %get-tuple-element.13, f32[3,256]{1,0:T(4,128)S(1)} %get-tuple-element.12, pred[256,4096]{1,0:T(8,128)(4,1)S(1)} %iota_compare_fusion, pred[3,4096]{1,0:T(4,128)(4,1)S(1)} %broadcast_compare_fusion), kind=kLoop, calls=%fused_computation.5 | loop fusion | flops 15727872 | bytes 13649920 | tf_op jit(solution)/shard_map/reduce_sum | solution.py:38
  241.2 0.6 copy.23
  241.8 0.6 copy.22
  (9 shorter events, 0.1 us)
Async XLA Ops:
  7.2 190.6 %all-gather.2.cloned.1.call-start = ((), (), s32[]{:S(2)}) async-start(), calls=%async_computation.1 | async-start | bytes 26738688 | tf_op jit(solution)/shard_map/all_gather | solution.py:68
  197.8 10.5 %copy-start = (bf16[3,8,32,1024]{3,2,1,0:T(8,128)(2,1)S(1)}, bf16[3,8,32,1024]{3,2,1,0:T(8,128)(2,1)}, u32[]{:S(2)}) copy-start(bf16[3,8,32,1024]{3,2,1,0:T(8,128)(2,1)} %copy.21) | copy-start | bytes 4718596
Sparse Core Ops, SparseCore 0:
  42.7 155.0 all-gather.1
where the time goes:
time: 250 us; the launch traced here: 249 us
  waiting for transfers between devices  154 us (62%)
  blocking collectives  26.5 us (11%)
  matrix products  25.9 us (10%)
  other arithmetic  25.6 us (10%)
  between operations  14.1 us (6%)
  local copies, waits for them, and re-layouts  3.03 us (1%)
    all_gather x1, waiting for transfers between devices, shards(): piece = lax.all_gather(received, 'dev', axis=1, tiled=True)  154 us
    all_to_all x1, blocking collectives, shards(): lax.all_to_all(outgoing, 'group', split_axis=1, concat_axis=1, tiled=True)  26.5 us
    dot_general x1, matrix products, tile_scores(): jnp.einsum('csd,cpd->csp', mine, partner, preferred_element_type=jnp.floa...  25.9 us
    reduce_sum x2, other arithmetic, presence(): return jnp.sum(jnp.square(blocks.astype(jnp.float32)), axis=-1) > 0.5  10.8 us
    reduce_sum x1, other arithmetic, reduce_tile(): jnp.sum(jnp.where(retained_rows, jnp.exp((similarity_scores - anchor) / S...  7.05 us
  transfers between devices with their start and end apart: 1, of which 1 were waited for; matrix products, arithmetic and copies ran while one was open for 0% of the time, Pallas kernels for 0%

commit v1 on v0

v1 whole, which is shorter than its diff:
```python
import functools
import math

import jax
import jax.numpy as jnp
from jax import lax
from jax.experimental import pallas as pl
from jax.experimental.pallas import tpu as pltpu
from jax.sharding import PartitionSpec as P

MESH = pl.DeviceIdType.MESH
SHARP = 20.0 * math.log2(math.e)
ABSENT = -1e30
COLS = ((0, 384), (384, 768), (768, 1024))
HALVES = 2


def mod4(value):
    return lax.rem(value + 16, 4)


def place():
    g = lax.axis_index("group")
    d = lax.axis_index("dev")
    return lax.rem(d, 4), g // 2, d // 4, lax.rem(g, 2)


def device(x, y, z, core):
    return (y * 2 + core, z * 4 + x)


def root_of(g, l):
    y = g // 2
    if l < 2:
        x = lax.rem(g, 2) * 2 + l
        return x, y, mod4(x + y)
    x = mod4(y - lax.rem(g, 2))
    return x, y, mod4(x + y + 2)


def slot_positions(own):
    g = (own * 11) >> 5
    l = own - 3 * g
    y = g >> 1
    odd = g & 1
    second = l == 2
    x = jnp.where(second, (y - odd) & 3, odd * 2 + l)
    z = jnp.where(second, x + y + 2, x + y) & 3
    return (
        x * 6 + jnp.where(second, 4 + odd, y),
        y * 6 + jnp.where(second, 5 - odd, z),
        z * 6 + jnp.where(second, 4 + (x >> 1), x),
    )


class Order:
    def __init__(self, kind, x, y, z, core):
        self.kind = kind
        self.a, self.b, self.c = ((x, y, z), (y, z, x), (z, x, y))[kind]
        self.core = core

    def at(self, a, b, c):
        x, y, z = ((a, b, c), (c, a, b), (b, c, a))[self.kind]
        return device(x, y, z, self.core)

    def first(self, a, b):
        return mod4((a + b, b - a, a - b)[self.kind])

    def has_second(self, a, b):
        if self.kind == 0:
            return mod4(b - a) < 2
        if self.kind == 1:
            return mod4(b - 2 * a - 1) < 2
        return (a < 2) == (lax.rem(b, 2) == 1)

    def second_slot(self, a, b):
        return 4 + (mod4(b - a), mod4(b - 2 * a - 1), b // 2)[self.kind]


def kernel(
    embeds, cid, owner, near_out, lse_out,
    raw, unit, pk0, pk1, pk2, ra0, ra1, ra2, rb0, rb1, rb2, rows, bias, flags, high, total, stats, landed,
    in_sem, s1, r1, c1, s2, r2, c2, s3, r3, c3, sx, rx, so, ro, co,
):
    x, y, z, core = place()
    pk, ra, rb = (pk0, pk1, pk2), (ra0, ra1, ra2), (rb0, rb1, rb2)
    orders = [Order(kind, x, y, z, core) for kind in range(3)]
    is_first = z == mod4(x + y)
    is_second = (z == mod4(x + y + 2)) & (mod4(y - x) < 2)
    is_root = is_first | is_second
    root_g = jnp.where(is_first, 2 * y + x // 2, 2 * y + mod4(y - x))
    root_l = jnp.where(is_first, lax.rem(x, 2), 2)
    peer = device(x, y, z, 1 - core)

    fetch = pltpu.make_async_copy(embeds, raw, in_sem)
    fetch.start()

    barrier = pltpu.get_barrier_semaphore()

    def greet(target):
        pl.semaphore_signal(barrier, inc=1, device_id=target, device_id_type=MESH)

    for step in (1, 2, 3):
        greet(device(mod4(x + step), y, z, core))
        greet(device(x, mod4(y + step), z, core))
        greet(device(x, y, mod4(z + step), core))
    greet(peer)
    g = lax.axis_index("group")
    for l in range(3):
        qx, qy, qz = root_of(g, l)
        for k in range(2):
            @pl.when((qx != x) | (qy != y) | (qz != z) | (core != k))
            def _():
                greet(device(qx, qy, qz, k))

    n = raw.shape[0]
    ids = cid[...]
    own = jnp.zeros_like(ids)
    for c in range(24):
        own = jnp.where(ids == c, owner[c], own)
    member = (lax.broadcasted_iota(jnp.int32, (32, n), 0) == ids).astype(jnp.float32)
    earlier = lax.broadcasted_iota(jnp.int32, (n, n), 0) < lax.broadcasted_iota(jnp.int32, (n, n), 1)
    before = jnp.dot(
        member.astype(jnp.bfloat16), earlier.astype(jnp.float32).astype(jnp.bfloat16), preferred_element_type=jnp.float32
    )
    rank = jnp.sum(member * before, axis=0, keepdims=True).astype(jnp.int32)
    spots = [slot * 16 + (rank & 15) + (rank >> 4) * 384 for slot in slot_positions(own)]

    fetch.wait()
    wide = raw[...].astype(jnp.float32)
    scale = lax.rsqrt(jnp.sum(wide * wide, axis=1, keepdims=True) + 1e-6)
    unit[...] = (wide * scale).astype(jnp.bfloat16)

    targets = lax.broadcasted_iota(jnp.int32, (384, n), 0)
    for half in range(HALVES):
        for kind, (lo, hi) in enumerate(COLS):
            pick = (targets == spots[kind] - half * 384).astype(jnp.float32).astype(jnp.bfloat16)
            moved = jnp.dot(pick, unit[:, lo:hi], preferred_element_type=jnp.float32)
            pk[kind][half] = moved.astype(jnp.bfloat16).reshape(4, 6, 16, hi - lo)

    extra = jnp.where(core == lax.rem(root_g, 2), 15, 16)
    pl.semaphore_wait(barrier, 10 + jnp.where(is_root, extra, 0))

    def remote(src, dst, send, recv, target):
        return pltpu.make_async_remote_copy(
            src_ref=src, dst_ref=dst, send_sem=send, recv_sem=recv, device_id=target, device_id_type=MESH
        )

    def drain(ref, sem):
        pltpu.make_async_copy(ref, ref, sem).wait()

    for half in range(HALVES):
        for kind, order in enumerate(orders):
            a, b, c = order.a, order.b, order.c
            for step in (1, 2, 3):
                to = mod4(a + step)
                remote(
                    pk[kind].at[half, to], ra[kind].at[half, a], s1.at[kind, half], r1.at[kind, half], order.at(to, b, c)
                ).start()
            pltpu.make_async_copy(pk[kind].at[half, a], ra[kind].at[half, a], c1.at[kind, half]).start()

    def landing(kind, which, half, b):
        return rb[kind].at[which, half, :, b] if kind == 2 else rb[kind].at[which, half, b]

    for half in range(HALVES):
        for kind, order in enumerate(orders):
            a, b, c = order.a, order.b, order.c
            drain(ra[kind].at[half, pl.ds(0, 3)], r1.at[kind, half])
            drain(ra[kind].at[half, 0], c1.at[kind, half])
            for step in (1, 2, 3):
                to = mod4(b + step)
                remote(
                    ra[kind].at[half, :, to], landing(kind, 0, half, b),
                    s2.at[kind, half, 0], r2.at[kind, half, 0], order.at(a, to, c),
                ).start()

                @pl.when(order.has_second(a, to))
                def _():
                    remote(
                        ra[kind].at[half, :, order.second_slot(a, to)], landing(kind, 1, half, b),
                        s2.at[kind, half, 1], r2.at[kind, half, 1], order.at(a, to, c),
                    ).start()

            pltpu.make_async_copy(ra[kind].at[half, :, b], landing(kind, 0, half, b), c2.at[kind, half, 0]).start()

            @pl.when(order.has_second(a, b))
            def _():
                pltpu.make_async_copy(
                    ra[kind].at[half, :, order.second_slot(a, b)], landing(kind, 1, half, b), c2.at[kind, half, 1]
                ).start()

    def final(kind, half, c):
        lo, hi = COLS[kind]
        if kind == 0:
            return rows.at[0, half, c, :, :, :, pl.ds(lo, hi - lo)]
        if kind == 1:
            return rows.at[0, half, :, :, c, :, pl.ds(lo, hi - lo)]
        return rows.at[0, half, :, c, :, :, pl.ds(lo, hi - lo)]

    for half in range(HALVES):
        for kind, order in enumerate(orders):
            a, b, c = order.a, order.b, order.c

            def pass_on(which):
                drain(rb[kind].at[which, half, pl.ds(0, 3)], r2.at[kind, half, which])
                drain(rb[kind].at[which, half, 0], c2.at[kind, half, which])
                to = mod4(order.first(a, b) + 2 * which)

                @pl.when(c != to)
                def _():
                    remote(
                        rb[kind].at[which, half], final(kind, half, c), s3.at[kind, half, which], r3.at[kind, half],
                        order.at(a, b, to),
                    ).start()

                @pl.when(c == to)
                def _():
                    pltpu.make_async_copy(rb[kind].at[which, half], final(kind, half, c), c3.at[kind, half]).start()

            pass_on(0)

            @pl.when(order.has_second(a, b))
            def _():
                pass_on(1)

    eye = lax.broadcasted_iota(jnp.int32, (256, 256), 0) == lax.broadcasted_iota(jnp.int32, (256, 256), 1)

    def block(which, half, part):
        return rows[which, half, part].reshape(256, 1024)

    def scores(left, right):
        return lax.dot_general(left, right, (((1,), (1,)), ((), ())), preferred_element_type=jnp.float32)

    def gather(values, half, part):
        shaped = values.reshape(32, 8, 256)
        high[half, part] = jnp.maximum(high[half, part], jnp.max(shaped, axis=0))
        total[half, part] = total[half, part] + jnp.sum(jnp.exp2(shaped), axis=0)

    def prepare(which, half):
        @pl.loop(0, 4)
        def _(part):
            me = block(which, half, part)
            score = scores(me, me)
            own_score = jnp.where(eye, score, 0.0)
            there = jnp.where(jnp.sum(own_score, axis=1, keepdims=True) > 0.5, -SHARP, ABSENT)
            spread = jnp.broadcast_to(there, (256, 256))
            bias[which, half, part] = spread
            if which == 0:
                flags[half, part] = jnp.sum(own_score.reshape(32, 8, 256), axis=0)
                gather(jnp.where(eye, ABSENT, score * SHARP + spread), half, part)

    def pairs(which, half, other):
        @pl.loop(0, 4)
        def _(part):
            left = block(which, half, part)
            spread = bias[which, half, part]

            def one(target):
                gather(scores(left, block(0, other, target)) * SHARP + spread, other, target)

            if which == 0 and half == other:
                for step in (1, 2, 3):
                    one(mod4(part + step))
            else:
                for target in range(4):
                    one(target)

    @pl.when(is_root)
    def _():
        high[...] = jnp.full(high.shape, ABSENT, jnp.float32)
        total[...] = jnp.zeros(total.shape, jnp.float32)
        for half in range(HALVES):
            for kind in range(3):
                drain(rb[kind].at[0, half, pl.ds(0, 3)], r3.at[kind, half]) if False else None
                lo, hi = COLS[kind]
                drain(rows.at[0, half, pl.ds(0, 3), :, :, :, pl.ds(lo, hi - lo)], r3.at[kind, half])
                drain(rows.at[0, half, 0, :, :, :, pl.ds(lo, hi - lo)], c3.at[kind, half])
            remote(rows.at[0, half], rows.at[1, half], sx.at[half], rx.at[half], peer).start()
            prepare(0, half)
            for other in range(half + 1):
                pairs(0, half, other)
                if other != half:
                    pairs(0, other, half)
            drain(rows.at[1, half], rx.at[half])
            prepare(1, half)
            for other in range(half + 1):
                pairs(1, half, other)
                if other != half:
                    pairs(1, other, half)
        for half in range(HALVES):
            for part in range(4):
                present = jnp.sum(flags[half, part], axis=0, keepdims=True) > 0.5
                top = jnp.max(high[half, part], axis=0, keepdims=True)
                mass = jnp.sum(total[half, part], axis=0, keepdims=True)
                paired = present & (top > 0.5 * ABSENT)
                near = jnp.where(paired, top * (1.0 / SHARP) + 1.0, -2.0)
                stats[part, half : half + 1] = jnp.where(present, near, 0.0)
                stats[part, 2 + half : 3 + half] = jnp.where(paired, 20.0 + jnp.log(jnp.where(paired, mass, 1.0)), 0.0)
        spot = root_l * 2 + core
        for part in range(4):
            for column in range(4):
                target = device(column, root_g // 2, part, lax.rem(root_g, 2))
                same = (x == column) & (z == part) & (core == lax.rem(root_g, 2))

                @pl.when(jnp.logical_not(same))
                def _():
                    remote(stats.at[part], landed.at[spot], so, ro, target).start()

                @pl.when(same)
                def _():
                    copy = pltpu.make_async_copy(stats.at[part], landed.at[spot], co)
                    copy.start()
                    copy.wait()

    in_mine = jnp.int32(0)
    for l in range(3):
        qx, qy, qz = root_of(g, l)
        in_mine = in_mine + jnp.where((qx == x) & (qy == y) & (qz == z), 1, 0)

    @pl.when(in_mine == 0)
    def _():
        drain(landed, ro)

    @pl.when(in_mine != 0)
    def _():
        drain(landed.at[pl.ds(0, 5)], ro)

    lane = lax.broadcasted_iota(jnp.int32, (8, 256), 1)
    keep = lax.rem(lane, 64) < 16
    for l in range(3):
        near = jnp.zeros((1, 256), jnp.float32)
        lse = jnp.zeros((1, 256), jnp.float32)
        for k in range(2):
            mine = jnp.where(keep, pltpu.roll(landed[2 * l + k], lax.rem(256 - 16 * x, 256), 1), 0.0)
            for half in range(HALVES):
                shift = k * 32 + half * 16
                moved = pltpu.roll(mine, shift, 1) if shift else mine
                near = near + moved[half : half + 1]
                lse = lse + moved[2 + half : 3 + half]
        near_out[l : l + 1] = near
        lse_out[l : l + 1] = lse

    for half in range(HALVES):
        for kind, order in enumerate(orders):
            a, b, c = order.a, order.b, order.c
            drain(pk[kind].at[half, pl.ds(0, 3)], s1.at[kind, half])
            drain(rb[kind].at[0, half, pl.ds(0, 3)], s2.at[kind, half, 0])
            for step in (1, 2, 3):
                @pl.when(order.has_second(a, mod4(b + step)))
                def _():
                    drain(rb[kind].at[1, half, 0], s2.at[kind, half, 1])

            @pl.when(c != order.first(a, b))
            def _():
                drain(rb[kind].at[0, half], s3.at[kind, half, 0])

            @pl.when(order.has_second(a, b) & (c != mod4(order.first(a, b) + 2)))
            def _():
                drain(rb[kind].at[1, half], s3.at[kind, half, 1])

    @pl.when(is_root)
    def _():
        for half in range(HALVES):
            drain(rows.at[0, half], sx.at[half])
        for count in range(15):
            drain(stats.at[0], so)

        @pl.when(core != lax.rem(root_g, 2))
        def _():
            drain(stats.at[0], so)


def solution(mesh):
    def step(embeds, cluster_id, owner_slot):
        n, width = embeds.shape
        bf, f32 = jnp.bfloat16, jnp.float32
        widths = [hi - lo for lo, hi in COLS]
        vmem = pltpu.VMEM
        dma = pltpu.SemaphoreType.DMA
        near, lse = pl.pallas_call(
            kernel,
            out_shape=[jax.ShapeDtypeStruct((3, 256), f32)] * 2,
            in_specs=[
                pl.BlockSpec(memory_space=pl.ANY),
                pl.BlockSpec(memory_space=pltpu.VMEM),
                pl.BlockSpec(memory_space=pltpu.SMEM),
            ],
            out_specs=[pl.BlockSpec(memory_space=pltpu.VMEM)] * 2,
            scratch_shapes=[vmem((n, width), bf), vmem((n, width), bf)]
            + [vmem((2, 4, 6, 16, w), bf) for w in widths]
            + [vmem((2, 4, 6, 16, w), bf) for w in widths]
            + [vmem((2, 2, 4, 4, 16, w), bf) for w in widths]
            + [
                vmem((2, 2, 4, 4, 4, 16, width), bf),
                vmem((2, 2, 4, 256, 256), f32),
                vmem((2, 4, 8, 256), f32),
                vmem((2, 4, 8, 256), f32),
                vmem((2, 4, 8, 256), f32),
                vmem((4, 8, 256), f32),
                vmem((6, 8, 256), f32),
                dma, dma((3, 2)), dma((3, 2)), dma((3, 2)),
                dma((3, 2, 2)), dma((3, 2, 2)), dma((3, 2, 2)),
                dma((3, 2, 2)), dma((3, 2)), dma((3, 2)),
                dma((2,)), dma((2,)), dma, dma, dma,
            ],
            compiler_params=pltpu.CompilerParams(
                collective_id=0, has_side_effects=True, vmem_limit_bytes=56 * 1024 * 1024
            ),
        )(embeds, cluster_id.reshape(1, n), owner_slot)
        return near[None, None], lse[None, None]

    return jax.shard_map(
        step,
        mesh=mesh,
        in_specs=(P(("group", "dev"), None), P(("group", "dev")), P()),
        out_specs=(P("group", "dev", None, None), P("group", "dev", None, None)),
        check_vma=False,
    )
```

time: 250 us -> 80.2 us (0.32)
  waiting for transfers between devices: 154 us -> 0 us
  Pallas kernels: 0 us -> 76.1 us
  blocking collectives: 26.5 us -> 0 us
  matrix products: 25.9 us -> 0 us
  other arithmetic: 25.6 us -> 0 us
  between operations: 14.1 us -> 0.65 us
    all_gather x1 -> x0, waiting for transfers between devices: 154 us -> none  [shards(): piece = lax.all_gather(received, 'dev', axis=1, tiled=True)]
    pallas_call x0 -> x1, Pallas kernels: none -> 76.1 us  [step(): pl.pallas_call(kernel, out_shape=[jax.ShapeDtypeStruct((3, 256), f32)] *...]
    all_to_all x1 -> x0, blocking collectives: 26.5 us -> none  [shards(): lax.all_to_all(outgoing, 'group', split_axis=1, concat_axis=1, tiled=True)]
    dot_general x1 -> x0, matrix products: 25.9 us -> none  [tile_scores(): jnp.einsum('csd,cpd->csp', mine, partner, preferred_element_type=jnp.floa...]
    reduce_sum x5 -> x0, other arithmetic: 20 us -> none  [the longest x2 10.8 us: presence(): return jnp.sum(jnp.square(blocks.astype(jnp.float32)), axis=-1) > 0.5]
    scatter x1 -> x0, other arithmetic: 3.22 us -> none  [shards(): jnp.zeros((clusters * most_rows, width), jnp.bfloat16).at[position]]
  transfers between devices with their start and end apart: 1 -> 0, of which waited for: 1 -> 0; matrix products, arithmetic and copies ran while one was open for 0% -> 0% of each run, Pallas kernels for 0% -> 0%
where the time goes in v1:
time: 80.2 us; the launch traced here: 79.9 us
  Pallas kernels  76.1 us (95%)
  local copies, waits for them, and re-layouts  3.17 us (4%)
    pallas_call x1, Pallas kernels, step(): pl.pallas_call(kernel, out_shape=[jax.ShapeDtypeStruct((3, 256), f32)] *...  76.1 us
    unnamed x6, local copies, waits for them, and re-layouts  1.93 us

profile of v1, /device:TPU:1, one launch (start us, length us, event | category | flops | bytes accessed | tf_op | source)
XLA Modules:
  0.0 79.9 jit_solution(7905036431653742222)
XLA Ops:
  0.6 1.2 %reshape.7.cid = s32[1,384]{1,0:T(1,128)} reshape(s32[384]{0:T(512)} %param.4) | data formatting | bytes 3072 | tf_op jit(solution)/shard_map/reshape | solution.py:409
  1.9 76.1 %shard_map.50 = (f32[3,256]{1,0:T(4,128)}, f32[3,256]{1,0:T(4,128)}) custom-call(bf16[384,1024]{1,0:T(8,128)(2,1)} %embeds.1, s32[1,384]{1,0:T(1,128)} %reshape.7.cid, s32[24]{0:T(128)} %owner.1), custom_call_target="tpu_custom_call" | custom-call | tf_op jit(solution)/shard_map/pallas_call | solution.py:380
  78.0 0.0 copy-start.1
  78.0 0.7 copy-done.1
  78.7 0.0 copy-start
  78.7 0.6 copy.5
  79.3 0.1 copy-done
  79.4 0.6 copy.6
Async XLA Ops:
  78.0 0.7 copy-start.1
  78.7 0.7 copy-start

commit v2 on v1

v2 whole, which is shorter than its diff:
```python
import functools
import math

import jax
import jax.numpy as jnp
from jax import lax
from jax.experimental import pallas as pl
from jax.experimental.pallas import tpu as pltpu
from jax.sharding import PartitionSpec as P

MESH = pl.DeviceIdType.MESH
SHARP = 20.0 * math.log2(math.e)
ABSENT = -1e30
COLS = ((0, 384), (384, 768), (768, 1024))
HALVES = 2


def mod4(value):
    return lax.rem(value + 16, 4)


def place():
    g = lax.axis_index("group")
    d = lax.axis_index("dev")
    return lax.rem(d, 4), g // 2, d // 4, lax.rem(g, 2)


def device(x, y, z, core):
    return (y * 2 + core, z * 4 + x)


def root_of(g, l):
    y = g // 2
    if l < 2:
        x = lax.rem(g, 2) * 2 + l
        return x, y, mod4(x + y)
    x = mod4(y - lax.rem(g, 2))
    return x, y, mod4(x + y + 2)


def slot_positions(own):
    g = (own * 11) >> 5
    l = own - 3 * g
    y = g >> 1
    odd = g & 1
    second = l == 2
    x = jnp.where(second, (y - odd) & 3, odd * 2 + l)
    z = jnp.where(second, x + y + 2, x + y) & 3
    return (
        x * 6 + jnp.where(second, 4 + odd, y),
        y * 6 + jnp.where(second, 5 - odd, z),
        z * 6 + jnp.where(second, 4 + (x >> 1), x),
    )


class Order:
    def __init__(self, kind, x, y, z, core):
        self.kind = kind
        self.a, self.b, self.c = ((x, y, z), (y, z, x), (z, x, y))[kind]
        self.core = core

    def at(self, a, b, c):
        x, y, z = ((a, b, c), (c, a, b), (b, c, a))[self.kind]
        return device(x, y, z, self.core)

    def first(self, a, b):
        return mod4((a + b, b - a, a - b)[self.kind])

    def has_second(self, a, b):
        if self.kind == 0:
            return mod4(b - a) < 2
        if self.kind == 1:
            return mod4(b - 2 * a - 1) < 2
        return (a < 2) == (lax.rem(b, 2) == 1)

    def second_slot(self, a, b):
        return 4 + (mod4(b - a), mod4(b - 2 * a - 1), b // 2)[self.kind]


def kernel(
    embeds, cid, owner, near_out, lse_out,
    raw, unit, pk0, pk1, pk2, ra0, ra1, ra2, rb0, rb1, rb2, rows, shade, veil, high, total, side_high, side_total,
    swap, swapped, stats, landed,
    in_sem, s1, r1, c1, s2, r2, c2, s3, r3, c3, sx, rx, se, re, so, ro, co,
):
    x, y, z, core = place()
    pk, ra, rb = (pk0, pk1, pk2), (ra0, ra1, ra2), (rb0, rb1, rb2)
    orders = [Order(kind, x, y, z, core) for kind in range(3)]
    is_first = z == mod4(x + y)
    is_second = (z == mod4(x + y + 2)) & (mod4(y - x) < 2)
    is_root = is_first | is_second
    root_g = jnp.where(is_first, 2 * y + x // 2, 2 * y + mod4(y - x))
    root_l = jnp.where(is_first, lax.rem(x, 2), 2)
    peer = device(x, y, z, 1 - core)
    g = lax.axis_index("group")

    fetch = pltpu.make_async_copy(embeds, raw, in_sem)
    fetch.start()

    barrier = pltpu.get_barrier_semaphore()

    def greet(target):
        pl.semaphore_signal(barrier, inc=1, device_id=target, device_id_type=MESH)

    for step in (1, 2, 3):
        greet(device(mod4(x + step), y, z, core))
        greet(device(x, mod4(y + step), z, core))
        greet(device(x, y, mod4(z + step), core))
    greet(peer)

    n = raw.shape[0]
    ids = cid[...].reshape(1, n)
    own = jnp.zeros_like(ids)
    for c in range(24):
        own = jnp.where(ids == c, owner[c], own)
    member = (lax.broadcasted_iota(jnp.int32, (32, n), 0) == ids).astype(jnp.float32)
    earlier = lax.broadcasted_iota(jnp.int32, (n, n), 0) < lax.broadcasted_iota(jnp.int32, (n, n), 1)
    before = jnp.dot(
        member.astype(jnp.bfloat16), earlier.astype(jnp.float32).astype(jnp.bfloat16), preferred_element_type=jnp.float32
    )
    rank = jnp.sum(member * before, axis=0, keepdims=True).astype(jnp.int32)
    spots = [slot * 16 + (rank & 15) + (rank >> 4) * 384 for slot in slot_positions(own)]

    fetch.wait()
    wide = raw[...].astype(jnp.float32)
    scale = lax.rsqrt(jnp.sum(wide * wide, axis=1, keepdims=True) + 1e-6)
    unit[...] = (wide * scale).astype(jnp.bfloat16)

    targets = lax.broadcasted_iota(jnp.int32, (384, n), 0)
    for half in range(HALVES):
        for kind, (lo, hi) in enumerate(COLS):
            pick = (targets == spots[kind] - half * 384).astype(jnp.float32).astype(jnp.bfloat16)
            moved = jnp.dot(pick, unit[:, lo:hi], preferred_element_type=jnp.float32)
            pk[kind][half] = moved.astype(jnp.bfloat16).reshape(4, 6, 16, hi - lo)

    @pl.when(is_root)
    def _():
        high[...] = jnp.full(high.shape, ABSENT, jnp.float32)
        total[...] = jnp.zeros(total.shape, jnp.float32)
        side_high[...] = jnp.full(side_high.shape, ABSENT, jnp.float32)
        side_total[...] = jnp.zeros(side_total.shape, jnp.float32)

    pl.semaphore_wait(barrier, 10)

    def remote(src, dst, send, recv, target):
        return pltpu.make_async_remote_copy(
            src_ref=src, dst_ref=dst, send_sem=send, recv_sem=recv, device_id=target, device_id_type=MESH
        )

    def drain(ref, sem):
        pltpu.make_async_copy(ref, ref, sem).wait()

    for half in range(HALVES):
        for kind, order in enumerate(orders):
            a, b, c = order.a, order.b, order.c
            for step in (1, 2, 3):
                to = mod4(a + step)
                remote(
                    pk[kind].at[half, to], ra[kind].at[half, a // 2, lax.rem(a, 2)],
                    s1.at[kind, half], r1.at[kind, half], order.at(to, b, c),
                ).start()
            pltpu.make_async_copy(
                pk[kind].at[half, a], ra[kind].at[half, a // 2, lax.rem(a, 2)], c1.at[kind, half]
            ).start()

    def landing(kind, which, half, b):
        if kind == 2:
            return rb[kind].at[which, half, :, :, b // 2, lax.rem(b, 2)]
        return rb[kind].at[which, half, b // 2, lax.rem(b, 2)]

    def second_phase(half):
        for kind, order in enumerate(orders):
            a, b, c = order.a, order.b, order.c
            drain(pk[kind].at[half, pl.ds(0, 3)], r1.at[kind, half])
            drain(pk[kind].at[half, 0], c1.at[kind, half])
            for step in (1, 2, 3):
                to = mod4(b + step)
                remote(
                    ra[kind].at[half, :, :, to], landing(kind, 0, half, b),
                    s2.at[kind, half, 0], r2.at[kind, half, 0], order.at(a, to, c),
                ).start()

                @pl.when(order.has_second(a, to))
                def _():
                    remote(
                        ra[kind].at[half, :, :, order.second_slot(a, to)], landing(kind, 1, half, b),
                        s2.at[kind, half, 1], r2.at[kind, half, 1], order.at(a, to, c),
                    ).start()

            pltpu.make_async_copy(ra[kind].at[half, :, :, b], landing(kind, 0, half, b), c2.at[kind, half, 0]).start()

            @pl.when(order.has_second(a, b))
            def _():
                pltpu.make_async_copy(
                    ra[kind].at[half, :, :, order.second_slot(a, b)], landing(kind, 1, half, b), c2.at[kind, half, 1]
                ).start()

    def piece(kind, which, q, low):
        lo, hi = COLS[kind]
        half, odd = q // 2, q % 2
        cols = pl.ds(lo, hi - lo)
        xl, yl, zl = lax.rem(x, 2), lax.rem(y, 2), lax.rem(z, 2)
        if kind == 0:
            other = lax.rem(odd + zl + low, 2)
            dst = rows.at[0, q, zl, low, z // 2, :, :, :, cols]
        elif kind == 1:
            other = lax.rem(odd + xl + low, 2)
            dst = rows.at[0, q, low, other, :, :, x // 2, :, cols]
        else:
            other = lax.rem(odd + yl + low, 2)
            dst = rows.at[0, q, low, yl, :, y // 2, :, :, cols]
        return rb[kind].at[which, half, :, low, :, other], dst

    def sends(kind, which):
        order = orders[kind]
        to = mod4(order.first(order.a, order.b) + 2 * which)
        return order.c != to, to

    def third_phase(q):
        half = q // 2
        for kind, order in enumerate(orders):
            a, b = order.a, order.b

            def pass_on(which):
                if q % 2 == 0:
                    drain(pk[kind].at[half, pl.ds(0, 2)], r2.at[kind, half, which])
                    drain(rb[kind].at[0, 0, 0, 0], c2.at[kind, half, which])
                away, to = sends(kind, which)

                @pl.when(away)
                def _():
                    if q:
                        @pl.when(jnp.logical_not(is_root))
                        def _():
                            drain(rb[kind].at[0, 0, 0], s3.at[kind, which, q - 1])


                    for low in range(2):
                        src, dst = piece(kind, which, q, low)
                        remote(src, dst, s3.at[kind, which, q], r3.at[kind, q], order.at(a, b, to)).start()

                @pl.when(jnp.logical_not(away))
                def _():
                    for low in range(2):
                        src, dst = piece(kind, which, q, low)
                        pltpu.make_async_copy(src, dst, c3.at[kind, q]).start()

            pass_on(0)

            @pl.when(order.has_second(a, b))
            def _():
                pass_on(1)

    eye = lax.broadcasted_iota(jnp.int32, (256, 256), 0) == lax.broadcasted_iota(jnp.int32, (256, 256), 1)

    def block(which, q, part):
        return rows[which, q, part].reshape(256, 1024)

    def chunk(which, q):
        return rows[which, q].reshape(512, 1024)

    def scores(left, right):
        return lax.dot_general(left, right, (((1,), (1,)), ((), ())), preferred_element_type=jnp.float32)

    def by_column(which, q, part, level, cols, power):
        shaped = level.shape[0] // 8, 8, 128
        high[which, q, part, :, cols] = jnp.maximum(high[which, q, part, :, cols], jnp.max(level.reshape(shaped), axis=0))
        total[which, q, part, :, cols] = total[which, q, part, :, cols] + jnp.sum(power.reshape(shaped), axis=0)

    def both_ways(left, right, own_q, lines, which, q, part):
        score = scores(left, right)
        row_veil = shade[own_q, lines]
        levels, powers = [], []
        for lane in range(2):
            cols = slice(lane * 128, lane * 128 + 128)
            level = score[:, cols] * SHARP + (row_veil + veil[which, q, part, 0:1, cols])
            power = jnp.exp2(level)
            by_column(which, q, part, level, cols, power)
            levels.append(level)
            powers.append(power)
        side_high[own_q, lines] = jnp.maximum(side_high[own_q, lines], jnp.maximum(levels[0], levels[1]))
        side_total[own_q, lines] = side_total[own_q, lines] + (powers[0] + powers[1])

    def own_pairs(q):
        me = chunk(0, q)
        score = [scores(me, block(0, q, part)) for part in range(2)]
        for part in range(2):
            square = jnp.where(eye, score[part][part * 256 : part * 256 + 256], 0.0)
            there = jnp.where(jnp.sum(square, axis=1, keepdims=True) > 0.5, 0.0, ABSENT)
            shade[q, part * 256 : part * 256 + 256] = jnp.broadcast_to(there, (256, 128))
            seen = jnp.sum(square, axis=0, keepdims=True) > 0.5
            veil[0, q, part] = jnp.broadcast_to(jnp.where(seen, -SHARP, ABSENT), (8, 256))
        for part in range(2):
            for lane in range(2):
                cols = slice(lane * 128, lane * 128 + 128)
                level = score[part][:, cols] * SHARP + (shade[q] - SHARP)
                here = level[part * 256 : part * 256 + 256]
                here = jnp.where(eye[:, cols], ABSENT, here)
                rest = level[256 - part * 256 : 512 - part * 256]
                by_column(0, q, part, here, cols, jnp.exp2(here))
                by_column(0, q, part, rest, cols, jnp.exp2(rest))
        if q:
            @pl.loop(0, q)
            def _(old):
                left = chunk(0, old)
                for part in range(2):
                    both_ways(left, block(0, q, part), old, slice(0, 512), 0, q, part)

    def cross_pairs(q):
        for part in range(2):
            right = block(1, q, part)
            square = jnp.where(eye, scores(right, right), 0.0)
            seen = jnp.sum(square, axis=0, keepdims=True) > 0.5
            veil[1, q, part] = jnp.broadcast_to(jnp.where(seen, -SHARP, ABSENT), (8, 256))
        for mine in range(2):
            part = lax.rem(mine + core, 2)
            both_ways(
                block(0, q, mine), block(1, q, part), q, slice(mine * 256, mine * 256 + 256), 1, q, part
            )
        if q:
            @pl.loop(0, q)
            def _(old):
                left = chunk(0, old)
                for part in range(2):
                    both_ways(left, block(1, q, part), old, slice(0, 512), 1, q, part)

    def arrive(q):
        for kind in range(3):
            drain(pk[kind].at[0], r3.at[kind, q])
            drain(rb[kind].at[0, 0, 0], c3.at[kind, q])
        remote(rows.at[0, q], rows.at[1, q], sx.at[q], rx.at[q], peer).start()

    def process(q):
        arrive(q)
        own_pairs(q)
        drain(rows.at[1, q], rx.at[q])
        cross_pairs(q)

    second_phase(0)
    for q in range(4):
        third_phase(q)
        if q == 0:
            second_phase(1)
        if q:
            @pl.when(is_root)
            def _():
                process(q - 1)

    @pl.when(is_root)
    def _():
        process(3)
        for q in range(4):
            for part in range(2):
                spot = 2 * q + part
                swap[0, spot : spot + 1] = jnp.max(high[1, q, part], axis=0, keepdims=True)
                swap[1, spot : spot + 1] = jnp.sum(total[1, q, part], axis=0, keepdims=True)
        remote(swap, swapped, se, re, peer).start()
        tops, masses = [], []
        for q in range(4):
            for part in range(2):
                lines = slice(part * 256, part * 256 + 256)
                side = jnp.max(side_high[q, lines].T.reshape(16, 8, 256), axis=0)
                tops.append(jnp.max(jnp.maximum(high[0, q, part], side), axis=0, keepdims=True))
                side = jnp.sum(side_total[q, lines].T.reshape(16, 8, 256), axis=0)
                masses.append(jnp.sum(total[0, q, part] + side, axis=0, keepdims=True))
        drain(swapped, re)
        for q in range(4):
            for part in range(2):
                spot = 2 * q + part
                present = veil[0, q, part, 0:1] > 0.5 * ABSENT
                top = jnp.maximum(tops[spot], swapped[0, spot : spot + 1])
                mass = masses[spot] + swapped[1, spot : spot + 1]
                paired = present & (top > 0.5 * ABSENT)
                near = jnp.where(paired, top * (1.0 / SHARP) + 1.0, -2.0)
                stats[part, q : q + 1] = jnp.where(present, near, 0.0)
                stats[part, 4 + q : 5 + q] = jnp.where(paired, 20.0 + jnp.log(jnp.where(paired, mass, 1.0)), 0.0)
        spot = root_l * 2 + core
        for row in range(4):
            for column in range(4):
                target = device(column, y, row, lax.rem(root_g, 2))
                same = (x == column) & (z == row) & (core == lax.rem(root_g, 2))

                @pl.when(jnp.logical_not(same))
                def _():
                    remote(stats.at[row % 2], landed.at[spot], so, ro, target).start()

                @pl.when(same)
                def _():
                    copy = pltpu.make_async_copy(stats.at[row % 2], landed.at[spot], co)
                    copy.start()
                    copy.wait()

    in_mine = jnp.int32(0)
    for l in range(3):
        qx, qy, qz = root_of(g, l)
        in_mine = in_mine + jnp.where((qx == x) & (qy == y) & (qz == z), 1, 0)

    @pl.when(in_mine == 0)
    def _():
        drain(landed, ro)

    @pl.when(in_mine != 0)
    def _():
        drain(landed.at[pl.ds(0, 5)], ro)

    lane = lax.broadcasted_iota(jnp.int32, (48, 256), 1)
    held = landed[...].reshape(48, 256)
    moved = []
    for odd in range(2):
        yl = lax.rem(odd + z + x, 2)
        kept = jnp.zeros((48, 256), jnp.float32)
        for yh in range(2):
            start = yl * 128 + (z // 2) * 64 + yh * 32 + (x // 2) * 16
            end = yh * 128 + yl * 64
            turned = pltpu.roll(held, lax.rem(end - start + 256, 256), 1)
            kept = kept + jnp.where((lane >= end) & (lane < end + 16), turned, 0.0)
        moved.append(kept)
    near = [jnp.zeros((1, 256), jnp.float32)] * 3
    lse = [jnp.zeros((1, 256), jnp.float32)] * 3
    for k in range(2):
        for half in range(HALVES):
            shift = k * 32 + half * 16
            for odd in range(2):
                turned = pltpu.roll(moved[odd], shift, 1) if shift else moved[odd]
                for l in range(3):
                    line = (2 * l + k) * 8 + half * 2 + odd
                    near[l] = near[l] + turned[line : line + 1]
                    lse[l] = lse[l] + turned[line + 4 : line + 5]
    for l in range(3):
        near_out[0, 0, l : l + 1] = near[l]
        lse_out[0, 0, l : l + 1] = lse[l]

    for half in range(HALVES):
        for kind, order in enumerate(orders):
            a, b, c = order.a, order.b, order.c
            drain(pk[kind].at[half, pl.ds(0, 3)], s1.at[kind, half])
            drain(pk[kind].at[half, pl.ds(0, 2)], s2.at[kind, half, 0])
            for step in (1, 2, 3):
                @pl.when(order.has_second(a, mod4(b + step)))
                def _():
                    drain(rb[kind].at[0, 0, 0, 0], s2.at[kind, half, 1])

    for kind, order in enumerate(orders):
        for which in range(2):
            away, _ = sends(kind, which)
            if which:
                away = away & order.has_second(order.a, order.b)

            @pl.when(away)
            def _():
                drain(rb[kind].at[0, 0, 0], s3.at[kind, which, 3])

                @pl.when(is_root)
                def _():
                    for q in range(3):
                        drain(rb[kind].at[0, 0, 0], s3.at[kind, which, q])

    @pl.when(is_root)
    def _():
        for q in range(4):
            drain(rows.at[0, q], sx.at[q])
        drain(swap, se)
        for count in range(15):
            drain(stats.at[0], so)

        @pl.when(core != lax.rem(root_g, 2))
        def _():
            drain(stats.at[0], so)


def solution(mesh):
    def step(embeds, cluster_id, owner_slot):
        n, width = embeds.shape
        bf, f32 = jnp.bfloat16, jnp.float32
        widths = [hi - lo for lo, hi in COLS]
        vmem = pltpu.VMEM
        dma = pltpu.SemaphoreType.DMA
        return pl.pallas_call(
            kernel,
            out_shape=[jax.ShapeDtypeStruct((1, 1, 3, 256), f32)] * 2,
            in_specs=[
                pl.BlockSpec(memory_space=pl.ANY),
                pl.BlockSpec(memory_space=pltpu.VMEM),
                pl.BlockSpec(memory_space=pltpu.SMEM),
            ],
            out_specs=[pl.BlockSpec(memory_space=pltpu.VMEM)] * 2,
            scratch_shapes=[vmem((n, width), bf), vmem((n, width), bf)]
            + [vmem((2, 4, 6, 16, w), bf) for w in widths]
            + [vmem((2, 2, 2, 6, 16, w), bf) for w in widths]
            + [vmem((2, 2, 2, 2, 2, 2, 16, w), bf) for w in widths]
            + [
                vmem((2, 4, 2, 2, 2, 2, 2, 16, width), bf),
                vmem((4, 512, 128), f32),
                vmem((2, 4, 2, 8, 256), f32),
                vmem((2, 4, 2, 8, 256), f32),
                vmem((2, 4, 2, 8, 256), f32),
                vmem((4, 512, 128), f32),
                vmem((4, 512, 128), f32),
                vmem((2, 8, 256), f32),
                vmem((2, 8, 256), f32),
                vmem((2, 8, 256), f32),
                vmem((6, 8, 256), f32),
                dma, dma((3, 2)), dma((3, 2)), dma((3, 2)),
                dma((3, 2, 2)), dma((3, 2, 2)), dma((3, 2, 2)),
                dma((3, 2, 4)), dma((3, 4)), dma((3, 4)),
                dma((4,)), dma((4,)), dma, dma, dma, dma, dma,
            ],
            compiler_params=pltpu.CompilerParams(
                collective_id=0, has_side_effects=True, vmem_limit_bytes=56 * 1024 * 1024
            ),
        )(embeds, cluster_id, owner_slot)

    return jax.shard_map(
        step,
        mesh=mesh,
        in_specs=(P(("group", "dev"), None), P(("group", "dev")), P()),
        out_specs=(P("group", "dev", None, None), P("group", "dev", None, None)),
        check_vma=False,
    )
```

time: 80.2 us -> 65 us (0.81)
  Pallas kernels: 76.1 us -> 62.3 us
  local copies, waits for them, and re-layouts: 3.17 us -> 1.84 us
    pallas_call x1, Pallas kernels: 76.1 us -> 62.3 us  [step(): pl.pallas_call(kernel, out_shape=[jax.ShapeDtypeStruct((1, 1, 3, 256), f3...]
    unnamed x6 -> x2, local copies, waits for them, and re-layouts: 1.93 us -> 0.01 us
    pallas_call x0 -> x2, local copies, waits for them, and re-layouts: none -> 1.83 us  [step(): pl.pallas_call(kernel, out_shape=[jax.ShapeDtypeStruct((1, 1, 3, 256), f3...]
    reshape x1 -> x0, local copies, waits for them, and re-layouts: 1.25 us -> none  [step(): cluster_id.reshape(1, n)]
where the time goes in v2:
time: 65 us; the launch traced here: 64.8 us
  Pallas kernels  62.3 us (96%)
  local copies, waits for them, and re-layouts  1.84 us (3%)
  between operations  0.65 us (1%)
    pallas_call x1, Pallas kernels, step(): pl.pallas_call(kernel, out_shape=[jax.ShapeDtypeStruct((1, 1, 3, 256), f3...  62.3 us
    pallas_call x2, local copies, waits for them, and re-layouts, step(): pl.pallas_call(kernel, out_shape=[jax.ShapeDtypeStruct((1, 1, 3, 256), f3...  1.83 us

profile of v2, /device:TPU:1, one launch (start us, length us, event | category | flops | bytes accessed | tf_op | source)
XLA Modules:
  0.0 64.8 jit_solution(6011070013146813737)
XLA Ops:
  0.6 62.3 %shard_map.50 = (f32[1,1,3,256]{3,2,1,0:T(4,128)}, f32[1,1,3,256]{3,2,1,0:T(4,128)}) custom-call(bf16[384,1024]{1,0:T(8,128)(2,1)} %embeds.1, s32[384]{0:T(512)} %cid.1, s32[24]{0:T(128)} %owner.1), custom_call_target="tpu_custom_call" | custom-call | tf_op jit(solution)/shard_map/pallas_call | solution.py:478
  63.0 0.0 copy-start
  63.0 1.3 %copy.5 = f32[1,1,3,256]{3,1,2,0:T(1,128)} copy(f32[1,1,3,256]{3,2,1,0:T(4,128)} %get-tuple-element.2) | data formatting | bytes 6144 | tf_op jit(solution)/shard_map/pallas_call | solution.py:478
  64.2 0.0 copy-done
  64.2 0.6 copy.6
Async XLA Ops:
  63.0 1.3 %copy-start = (f32[1,1,3,256]{3,2,1,0:T(4,128)S(1)}, f32[1,1,3,256]{3,2,1,0:T(4,128)}, u32[]{:S(2)}) copy-start(f32[1,1,3,256]{3,2,1,0:T(4,128)} %get-tuple-element.3) | copy-start | bytes 9220

commit v3 on v2

v3 whole, which is shorter than its diff:
```python
import functools
import math

import jax
import jax.numpy as jnp
from jax import lax
from jax.experimental import pallas as pl
from jax.experimental.pallas import tpu as pltpu
from jax.sharding import PartitionSpec as P

MESH = pl.DeviceIdType.MESH
SHARP = 20.0 * math.log2(math.e)
ABSENT = -1e30
COLS = ((0, 384), (384, 768), (768, 1024))
HALVES = 2


def mod4(value):
    return lax.rem(value + 16, 4)


def place():
    g = lax.axis_index("group")
    d = lax.axis_index("dev")
    return mod4(lax.rem(d, 4) + 0), mod4(g // 2 + 0), mod4(d // 4 + 1), lax.rem(g, 2)


def device(x, y, z, core):
    return (mod4(y - 0) * 2 + core, mod4(z - 1) * 4 + mod4(x - 0))


def root_of(g, l):
    y = g // 2
    if l < 2:
        x = lax.rem(g, 2) * 2 + l
        return x, y, mod4(x + y)
    x = mod4(y - lax.rem(g, 2))
    return x, y, mod4(x + y + 2)


def slot_positions(own):
    g = (own * 11) >> 5
    l = own - 3 * g
    y = g >> 1
    odd = g & 1
    second = l == 2
    x = jnp.where(second, (y - odd) & 3, odd * 2 + l)
    z = jnp.where(second, x + y + 2, x + y) & 3
    return (
        x * 6 + jnp.where(second, 4 + odd, y),
        y * 6 + jnp.where(second, 5 - odd, z),
        z * 6 + jnp.where(second, 4 + (x >> 1), x),
    )


class Order:
    def __init__(self, kind, x, y, z, core):
        self.kind = kind
        self.a, self.b, self.c = ((x, y, z), (y, z, x), (z, x, y))[kind]
        self.core = core

    def at(self, a, b, c):
        x, y, z = ((a, b, c), (c, a, b), (b, c, a))[self.kind]
        return device(x, y, z, self.core)

    def first(self, a, b):
        return mod4((a + b, b - a, a - b)[self.kind])

    def has_second(self, a, b):
        if self.kind == 0:
            return mod4(b - a) < 2
        if self.kind == 1:
            return mod4(b - 2 * a - 1) < 2
        return (a < 2) == (lax.rem(b, 2) == 1)

    def second_slot(self, a, b):
        return 4 + (mod4(b - a), mod4(b - 2 * a - 1), b // 2)[self.kind]


def kernel(
    embeds, cluster_id, owner_slot, both_out,
    raw, cid, owner, unit, pk0, pk1, pk2, ra0, ra1, ra2, rb0, rb1, rb2, rows, shade, veil, high, total, side_high, side_total, stats, landed,
    in_sem, id_sem, owner_sem, s1, r1, c1, s2, r2, c2, s3, r3, c3, sx, rx, sv, rv, so, ro, co,
):
    x, y, z, core = place()
    pk, ra, rb = (pk0, pk1, pk2), (ra0, ra1, ra2), (rb0, rb1, rb2)
    orders = [Order(kind, x, y, z, core) for kind in range(3)]
    is_first = z == mod4(x + y)
    is_second = (z == mod4(x + y + 2)) & (mod4(y - x) < 2)
    is_root = is_first | is_second
    root_g = jnp.where(is_first, 2 * y + x // 2, 2 * y + mod4(y - x))
    root_l = jnp.where(is_first, lax.rem(x, 2), 2)
    peer = device(x, y, z, 1 - core)
    g = lax.axis_index("group")

    barrier = pltpu.get_barrier_semaphore()

    def greet(target):
        pl.semaphore_signal(barrier, inc=1, device_id=target, device_id_type=MESH)

    for step in (1, 2, 3):
        greet(device(mod4(x + step), y, z, core))
        greet(device(x, mod4(y + step), z, core))
        greet(device(x, y, mod4(z + step), core))
    greet(peer)
    fetch = pltpu.make_async_copy(embeds, raw, in_sem)
    fetch_ids = pltpu.make_async_copy(cluster_id, cid, id_sem)
    fetch_owner = pltpu.make_async_copy(owner_slot, owner, owner_sem)
    fetch_ids.start()
    fetch_owner.start()
    fetch.start()

    n = raw.shape[0]
    fetch_ids.wait()
    fetch_owner.wait()
    ids = cid[...].reshape(1, n)
    own = jnp.zeros_like(ids)
    for c in range(24):
        own = jnp.where(ids == c, owner[c], own)
    member = (lax.broadcasted_iota(jnp.int32, (32, n), 0) == ids).astype(jnp.float32)
    earlier = lax.broadcasted_iota(jnp.int32, (n, n), 0) < lax.broadcasted_iota(jnp.int32, (n, n), 1)
    before = jnp.dot(
        member.astype(jnp.bfloat16), earlier.astype(jnp.float32).astype(jnp.bfloat16), preferred_element_type=jnp.float32
    )
    rank = jnp.sum(member * before, axis=0, keepdims=True).astype(jnp.int32)
    spots = [slot * 16 + (rank & 15) + (rank >> 4) * 384 for slot in slot_positions(own)]

    fetch.wait()
    wide = raw[...].astype(jnp.float32)
    scale = lax.rsqrt(jnp.sum(wide * wide, axis=1, keepdims=True) + 1e-6)
    unit[...] = (wide * scale).astype(jnp.bfloat16)

    targets = lax.broadcasted_iota(jnp.int32, (384, n), 0)
    for half in range(HALVES):
        for kind, (lo, hi) in enumerate(COLS):
            pick = (targets == spots[kind] - half * 384).astype(jnp.float32).astype(jnp.bfloat16)
            moved = jnp.dot(pick, unit[:, lo:hi], preferred_element_type=jnp.float32)
            pk[kind][half] = moved.astype(jnp.bfloat16).reshape(4, 6, 16, hi - lo)

    @pl.when(is_root)
    def _():
        high[...] = jnp.full(high.shape, ABSENT, jnp.float32)
        total[...] = jnp.zeros(total.shape, jnp.float32)
        side_high[...] = jnp.full(side_high.shape, ABSENT, jnp.float32)
        side_total[...] = jnp.zeros(side_total.shape, jnp.float32)

    pl.semaphore_wait(barrier, 10)

    def remote(src, dst, send, recv, target):
        return pltpu.make_async_remote_copy(
            src_ref=src, dst_ref=dst, send_sem=send, recv_sem=recv, device_id=target, device_id_type=MESH
        )

    def drain(ref, sem):
        pltpu.make_async_copy(ref, ref, sem).wait()

    def first_phase(half):
        for kind, order in enumerate(orders):
            a, b, c = order.a, order.b, order.c
            for step in (1, 2, 3):
                to = mod4(a + step)
                remote(
                    pk[kind].at[half, to], ra[kind].at[half, a // 2, lax.rem(a, 2)],
                    s1.at[kind, half], r1.at[kind, half], order.at(to, b, c),
                ).start()
            pltpu.make_async_copy(
                pk[kind].at[half, a], ra[kind].at[half, a // 2, lax.rem(a, 2)], c1.at[kind, half]
            ).start()

    def landing(kind, which, half, b):
        if kind == 2:
            return rb[kind].at[which, half, :, :, b // 2, lax.rem(b, 2)]
        return rb[kind].at[which, half, b // 2, lax.rem(b, 2)]

    def second_phase(half):
        for kind, order in enumerate(orders):
            a, b, c = order.a, order.b, order.c
            drain(pk[kind].at[half, pl.ds(0, 3)], r1.at[kind, half])
            drain(pk[kind].at[half, 0], c1.at[kind, half])
            for step in (1, 2, 3):
                to = mod4(b + step)
                remote(
                    ra[kind].at[half, :, :, to], landing(kind, 0, half, b),
                    s2.at[kind, half, 0], r2.at[kind, half, 0], order.at(a, to, c),
                ).start()

                @pl.when(order.has_second(a, to))
                def _():
                    remote(
                        ra[kind].at[half, :, :, order.second_slot(a, to)], landing(kind, 1, half, b),
                        s2.at[kind, half, 1], r2.at[kind, half, 1], order.at(a, to, c),
                    ).start()

            pltpu.make_async_copy(ra[kind].at[half, :, :, b], landing(kind, 0, half, b), c2.at[kind, half, 0]).start()

            @pl.when(order.has_second(a, b))
            def _():
                pltpu.make_async_copy(
                    ra[kind].at[half, :, :, order.second_slot(a, b)], landing(kind, 1, half, b), c2.at[kind, half, 1]
                ).start()

    def piece(kind, which, q, low):
        lo, hi = COLS[kind]
        half, odd = q // 2, q % 2
        cols = pl.ds(lo, hi - lo)
        xl, yl, zl = lax.rem(x, 2), lax.rem(y, 2), lax.rem(z, 2)
        if kind == 0:
            other = lax.rem(odd + zl + low, 2)
            dst = rows.at[0, q, zl, z // 2, low, :, :, :, cols]
        elif kind == 1:
            other = lax.rem(odd + xl + low, 2)
            dst = rows.at[0, q, low, :, other, :, x // 2, :, cols]
        else:
            other = lax.rem(odd + yl + low, 2)
            dst = rows.at[0, q, low, :, yl, y // 2, :, :, cols]
        return rb[kind].at[which, half, :, low, :, other], dst

    def sends(kind, which):
        order = orders[kind]
        to = mod4(order.first(order.a, order.b) + 2 * which)
        return order.c != to, to

    def third_phase(q):
        half = q // 2
        for kind, order in enumerate(orders):
            a, b = order.a, order.b

            def pass_on(which):
                if q % 2 == 0:
                    drain(pk[kind].at[half, pl.ds(0, 2)], r2.at[kind, half, which])
                    drain(rb[kind].at[0, 0, 0, 0], c2.at[kind, half, which])
                away, to = sends(kind, which)

                @pl.when(away)
                def _():
                    for low in range(2):
                        if q:
                            @pl.when(jnp.logical_not(is_root))
                            def _():
                                drain(rb[kind].at[0, 0, 0, 0], s3.at[kind, which, q - 1, low])

                        src, dst = piece(kind, which, q, low)
                        remote(src, dst, s3.at[kind, which, q, low], r3.at[kind, q], order.at(a, b, to)).start()

                @pl.when(jnp.logical_not(away))
                def _():
                    for low in range(2):
                        src, dst = piece(kind, which, q, low)
                        pltpu.make_async_copy(src, dst, c3.at[kind, q]).start()

            pass_on(0)

            @pl.when(order.has_second(a, b))
            def _():
                pass_on(1)

    eye = lax.broadcasted_iota(jnp.int32, (256, 256), 0) == lax.broadcasted_iota(jnp.int32, (256, 256), 1)

    def block(which, q, part):
        return rows[which, q, part].reshape(256, 1024)

    def chunk(which, q):
        return rows[which, q].reshape(512, 1024)

    def scores(left, right):
        return lax.dot_general(left, right, (((1,), (1,)), ((), ())), preferred_element_type=jnp.float32)

    strip = 64

    def fold(values, merge):
        return merge(values.reshape(values.shape[0] // 8, 8, 128), axis=0)

    def merge_columns(which, q, part, tops, masses):
        for lane in range(2):
            cols = slice(lane * 128, lane * 128 + 128)
            high[which, q, part, :, cols] = jnp.maximum(high[which, q, part, :, cols], tops[lane])
            total[which, q, part, :, cols] = total[which, q, part, :, cols] + masses[lane]

    def both_ways(left, right, own_q, first, which, q, part):
        score = scores(left, right)
        tops, masses = [None, None], [None, None]
        for row in range(0, left.shape[0], strip):
            lines = slice(first + row, first + row + strip)
            row_veil = shade[own_q, lines]
            levels, powers = [], []
            for lane in range(2):
                cols = slice(lane * 128, lane * 128 + 128)
                level = score[row : row + strip, cols] * SHARP + (row_veil + veil[which, q, part, 0:1, cols])
                power = jnp.exp2(level)
                top, mass = fold(level, jnp.max), fold(power, jnp.sum)
                tops[lane] = top if row == 0 else jnp.maximum(tops[lane], top)
                masses[lane] = mass if row == 0 else masses[lane] + mass
                levels.append(level)
                powers.append(power)
            side_high[own_q, lines] = jnp.maximum(side_high[own_q, lines], jnp.maximum(levels[0], levels[1]))
            side_total[own_q, lines] = side_total[own_q, lines] + (powers[0] + powers[1])
        merge_columns(which, q, part, tops, masses)

    def own_pairs(q):
        me = chunk(0, q)
        score = [scores(me, block(0, q, part)) for part in range(2)]
        for part in range(2):
            square = jnp.where(eye, score[part][part * 256 : part * 256 + 256], 0.0)
            there = jnp.where(jnp.sum(square, axis=1, keepdims=True) > 0.5, 0.0, ABSENT)
            shade[q, part * 256 : part * 256 + 256] = jnp.broadcast_to(there, (256, 128))
            seen = jnp.sum(square, axis=0, keepdims=True) > 0.5
            veil[0, q, part] = jnp.broadcast_to(jnp.where(seen, -SHARP, ABSENT), (8, 256))
        remote(veil.at[0, q], veil.at[1, q], sv.at[q], rv.at[q], peer).start()
        for part in range(2):
            tops, masses = [None, None], [None, None]
            for row in range(0, 512, strip):
                for lane in range(2):
                    cols = slice(lane * 128, lane * 128 + 128)
                    level = score[part][row : row + strip, cols] * SHARP + (shade[q, row : row + strip] - SHARP)
                    if row // 256 == part:
                        level = jnp.where(eye[row % 256 : row % 256 + strip, cols], ABSENT, level)
                    top, mass = fold(level, jnp.max), fold(jnp.exp2(level), jnp.sum)
                    tops[lane] = top if row == 0 else jnp.maximum(tops[lane], top)
                    masses[lane] = mass if row == 0 else masses[lane] + mass
            merge_columns(0, q, part, tops, masses)
        for old in range(q):
            left = chunk(0, old)
            for part in range(2):
                both_ways(left, block(0, q, part), old, 0, 0, q, part)

    def cross_pairs(q):
        for mine in range(2):
            part = lax.rem(mine + core, 2)
            both_ways(
                block(0, q, mine), block(1, q, part), q, mine * 256, 1, q, part
            )
        for old in range(q):
            left = chunk(0, old)
            for part in range(2):
                both_ways(left, block(1, q, part), old, 0, 1, q, part)

    def arrive(q):
        for kind in range(3):
            drain(pk[kind].at[0], r3.at[kind, q])
            drain(rb[kind].at[0, 0, 0], c3.at[kind, q])
            lo, hi = COLS[kind]
            cols = pl.ds(lo, hi - lo)
            remote(
                rows.at[0, q, :, :, :, :, :, :, cols], rows.at[1, q, :, :, :, :, :, :, cols],
                sx.at[kind, q], rx.at[kind, q], peer,
            ).start()

    def process(q):
        if q not in (2, 3):
            arrive(q)
        own_pairs(q)
        for kind in range(3):
            drain(rb[kind].at[0], rx.at[kind, q])
        drain(veil.at[1, q], rv.at[q])
        if q + 1 in (2, 3):
            arrive(q + 1)
        cross_pairs(q)

    first_phase(0)
    first_phase(1)
    second_phase(0)
    second_phase(1)
    third_phase(0)
    third_phase(1)
    third_phase(2)
    third_phase(3)

    @pl.when(is_root)
    def _():
        process(0)


    @pl.when(is_root)
    def _():
        process(1)


    @pl.when(is_root)
    def _():
        process(2)


    @pl.when(is_root)
    def _():
        process(3)
        for q in range(4):
            for part in range(2):
                lines = slice(part * 256, part * 256 + 256)
                side = jnp.max(side_high[q, lines].T.reshape(16, 8, 256), axis=0)
                top = jnp.max(jnp.maximum(high[0, q, part], side), axis=0, keepdims=True)
                top = jnp.where(veil[0, q, part, 0:1] > 0.5 * ABSENT, top, -ABSENT)
                side = jnp.sum(side_total[q, lines].T.reshape(16, 8, 256), axis=0)
                mass = jnp.sum(total[0, q, part] + side, axis=0, keepdims=True)
                far_top = jnp.max(high[1, q, part], axis=0, keepdims=True)
                far_mass = jnp.sum(total[1, q, part], axis=0, keepdims=True)
                for line, value in ((q, top), (4 + q, mass), (8 + q, far_top), (12 + q, far_mass)):
                    for lane in range(2):
                        stats[part, lane, line : line + 1] = value[:, lane * 128 : lane * 128 + 128]
        spot = root_l * 2 + core
        for step in range(16):
            row = mod4(z + step // 4)
            column = mod4(x + step % 4)
            target = device(column, y, row, lax.rem(root_g, 2))
            src = stats.at[lax.rem(row, 2), row // 2]
            if step:
                remote(src, landed.at[spot], so, ro, target).start()
            else:
                same = core == lax.rem(root_g, 2)

                @pl.when(jnp.logical_not(same))
                def _():
                    remote(src, landed.at[spot], so, ro, target).start()

                @pl.when(same)
                def _():
                    copy = pltpu.make_async_copy(src, landed.at[spot], co)
                    copy.start()
                    copy.wait()

    for half in range(HALVES):
        for kind, order in enumerate(orders):
            a, b, c = order.a, order.b, order.c
            drain(pk[kind].at[half, pl.ds(0, 3)], s1.at[kind, half])
            drain(pk[kind].at[half, pl.ds(0, 2)], s2.at[kind, half, 0])
            for step in (1, 2, 3):
                @pl.when(order.has_second(a, mod4(b + step)))
                def _():
                    drain(rb[kind].at[0, 0, 0, 0], s2.at[kind, half, 1])

    for kind, order in enumerate(orders):
        for which in range(2):
            away, _ = sends(kind, which)
            if which:
                away = away & order.has_second(order.a, order.b)

            @pl.when(away)
            def _():
                for low in range(2):
                    drain(rb[kind].at[0, 0, 0, 0], s3.at[kind, which, 3, low])

                @pl.when(is_root)
                def _():
                    for q in range(3):
                        for low in range(2):
                            drain(rb[kind].at[0, 0, 0, 0], s3.at[kind, which, q, low])

    @pl.when(is_root)
    def _():
        for q in range(4):
            for kind in range(3):
                drain(rb[kind].at[0], sx.at[kind, q])
            drain(veil.at[0, q], sv.at[q])
        for count in range(15):
            drain(stats.at[0, 0], so)

        @pl.when(core != lax.rem(root_g, 2))
        def _():
            drain(stats.at[0, 0], so)

    in_mine = jnp.int32(0)
    for l in range(3):
        qx, qy, qz = root_of(g, l)
        in_mine = in_mine + jnp.where((qx == x) & (qy == y) & (qz == z), 1, 0)

    @pl.when(in_mine == 0)
    def _():
        drain(landed, ro)

    @pl.when(in_mine != 0)
    def _():
        drain(landed.at[pl.ds(0, 5)], ro)

    lane = lax.broadcasted_iota(jnp.int32, (48, 128), 1)
    first = lax.broadcasted_iota(jnp.int32, (8, 128), 0) < 4
    final = []
    for l in range(3):
        for k in range(2):
            mine, other = landed[2 * l + k], landed[2 * l + 1 - k]
            top = jnp.maximum(mine[0:4], other[8:12])
            mass = mine[4:8] + other[12:16]
            top = jnp.concatenate([top, top], axis=0)
            mass = jnp.concatenate([mass, mass], axis=0)
            paired = top > 0.5 * ABSENT
            near_row = jnp.where(paired, top * (1.0 / SHARP) + 1.0, -2.0)
            lse_row = jnp.where(paired, 20.0 + jnp.log(jnp.where(paired, mass, 1.0)), 0.0)
            final.append(jnp.where(top > -0.5 * ABSENT, 0.0, jnp.where(first, near_row, lse_row)))
    held = jnp.concatenate(final, axis=0)
    out = [[jnp.zeros((1, 128), jnp.float32) for _ in range(6)] for _ in range(2)]
    for yh in range(2):
        turned = pltpu.roll(held, lax.rem(256 - yh * 32 - (x // 2) * 16, 128), 1)
        for odd in range(2):
            start = lax.rem(odd + z + x, 2) * 64
            kept = jnp.where((lane >= start) & (lane < start + 16), turned, 0.0)
            for k in range(2):
                for half in range(HALVES):
                    shift = k * 32 + half * 16
                    moved = pltpu.roll(kept, shift, 1) if shift else kept
                    for l in range(3):
                        line = (2 * l + k) * 8 + half * 2 + odd
                        out[yh][l] = out[yh][l] + moved[line : line + 1]
                        out[yh][3 + l] = out[yh][3 + l] + moved[line + 4 : line + 5]
        for which in range(2):
            for l in range(3):
                both_out[which, l, :, yh * 128 : yh * 128 + 128] = out[yh][3 * which + l]


def solution(mesh):
    def step(embeds, cluster_id, owner_slot):
        n, width = embeds.shape
        bf, f32 = jnp.bfloat16, jnp.float32
        widths = [hi - lo for lo, hi in COLS]
        vmem = pltpu.VMEM
        dma = pltpu.SemaphoreType.DMA
        both = pl.pallas_call(
            kernel,
            out_shape=jax.ShapeDtypeStruct((2, 3, 1, 256), f32),
            in_specs=[pl.BlockSpec(memory_space=pl.ANY)] * 3,
            out_specs=pl.BlockSpec(memory_space=pltpu.VMEM),
            scratch_shapes=[vmem((n, width), bf), vmem((n,), jnp.int32), pltpu.SMEM((24,), jnp.int32), vmem((n, width), bf)]
            + [vmem((2, 4, 6, 16, w), bf) for w in widths]
            + [vmem((2, 2, 2, 6, 16, w), bf) for w in widths]
            + [vmem((2, 2, 2, 2, 2, 2, 16, w), bf) for w in widths]
            + [
                vmem((2, 4, 2, 2, 2, 2, 2, 16, width), bf),
                vmem((4, 512, 128), f32),
                vmem((2, 4, 2, 8, 256), f32),
                vmem((2, 4, 2, 8, 256), f32),
                vmem((2, 4, 2, 8, 256), f32),
                vmem((4, 512, 128), f32),
                vmem((4, 512, 128), f32),
                vmem((2, 2, 16, 128), f32),
                vmem((6, 16, 128), f32),
                dma, dma, dma, dma((3, 2)), dma((3, 2)), dma((3, 2)),
                dma((3, 2, 2)), dma((3, 2, 2)), dma((3, 2, 2)),
                dma((3, 2, 4, 2)), dma((3, 4)), dma((3, 4)),
                dma((3, 4)), dma((3, 4)), dma((4,)), dma((4,)), dma, dma, dma,
            ],
            compiler_params=pltpu.CompilerParams(
                collective_id=0, has_side_effects=True, vmem_limit_bytes=56 * 1024 * 1024
            ),
        )(embeds, cluster_id, owner_slot)
        return both[0].reshape(1, 1, 3, 256), both[1].reshape(1, 1, 3, 256)

    return jax.shard_map(
        step,
        mesh=mesh,
        in_specs=(P(("group", "dev"), None), P(("group", "dev")), P()),
        out_specs=(P("group", "dev", None, None), P("group", "dev", None, None)),
        check_vma=False,
    )
```

time: 65 us -> 60 us (0.923)
  Pallas kernels: 62.3 us -> 57.9 us
    pallas_call x1, Pallas kernels: 62.3 us -> 57.9 us  [step(): pl.pallas_call(kernel, out_shape=jax.ShapeDtypeStruct((2, 3, 1, 256), f32...]
    pallas_call x2 -> x0, local copies, waits for them, and re-layouts: 1.83 us -> none  [step(): pl.pallas_call(kernel, out_shape=[jax.ShapeDtypeStruct((1, 1, 3, 256), f3...]
    unnamed x2 -> x1, local copies, waits for them, and re-layouts: 0.01 us -> 1.26 us
where the time goes in v3:
time: 60 us; the launch traced here: 59.8 us
  Pallas kernels  57.9 us (96%)
  local copies, waits for them, and re-layouts  1.26 us (2%)
  between operations  0.64 us (1%)
    pallas_call x1, Pallas kernels, step(): pl.pallas_call(kernel, out_shape=jax.ShapeDtypeStruct((2, 3, 1, 256), f32...  57.9 us
    unnamed x1, local copies, waits for them, and re-layouts  1.26 us

profile of v3, /device:TPU:1, one launch (start us, length us, event | category | flops | bytes accessed | tf_op | source)
XLA Modules:
  0.0 59.8 jit_solution(4675161810244803939)
XLA Ops:
  0.6 57.9 %shard_map.50 = f32[2,3,1,256]{3,2,1,0:T(1,128)} custom-call(bf16[384,1024]{1,0:T(8,128)(2,1)} %embeds.1, s32[384]{0:T(512)} %cluster_id.1, s32[24]{0:T(128)} %owner_slot.1), custom_call_target="tpu_custom_call" | custom-call | tf_op jit(solution)/shard_map/pallas_call | solution.py:514
  58.6 1.3 %slice_bitcast_fusion = (f32[1,1,3,256]{3,1,2,0:T(1,128)}, f32[1,1,3,256]{3,1,2,0:T(1,128)}) fusion(f32[2,3,1,256]{3,2,1,0:T(1,128)} %shard_map.50), kind=kLoop, calls=%fused_computation | loop fusion | bytes 12288

commit v4 on v3

--- a/solution.py
+++ b/solution.py
@@ -79,11 +79,11 @@
 
 def kernel(
     embeds, cluster_id, owner_slot, both_out,
-    raw, cid, owner, unit, pk0, pk1, pk2, ra0, ra1, ra2, rb0, rb1, rb2, rows, shade, veil, high, total, side_high, side_total, stats, landed,
-    in_sem, id_sem, owner_sem, s1, r1, c1, s2, r2, c2, s3, r3, c3, sx, rx, sv, rv, so, ro, co,
+    raw, cid, owner, unit, pk0, pk1, pk2, ra0, ra1, ra2, rb0, rb1, rb2, rl0, rl1, rl2, rows, shade, veil, high, total, side_high, side_total, stats, landed,
+    in_sem, id_sem, owner_sem, s1, r1, c1, s2, r2, c2, s3, r3, c3, s4, r4, sx, rx, sv, rv, so, ro, co,
 ):
     x, y, z, core = place()
-    pk, ra, rb = (pk0, pk1, pk2), (ra0, ra1, ra2), (rb0, rb1, rb2)
+    pk, ra, rb, rl = (pk0, pk1, pk2), (ra0, ra1, ra2), (rb0, rb1, rb2), (rl0, rl1, rl2)
     orders = [Order(kind, x, y, z, core) for kind in range(3)]
     is_first = z == mod4(x + y)
     is_second = (z == mod4(x + y + 2)) & (mod4(y - x) < 2)
@@ -199,20 +199,18 @@
                     ra[kind].at[half, :, :, order.second_slot(a, b)], landing(kind, 1, half, b), c2.at[kind, half, 1]
                 ).start()
 
-    def piece(kind, which, q, low):
+    def piece(kind, which, q, low, c):
         lo, hi = COLS[kind]
         half, odd = q // 2, q % 2
         cols = pl.ds(lo, hi - lo)
-        xl, yl, zl = lax.rem(x, 2), lax.rem(y, 2), lax.rem(z, 2)
+        cl, ch = lax.rem(c, 2), c // 2
+        other = lax.rem(odd + cl + low, 2)
         if kind == 0:
-            other = lax.rem(odd + zl + low, 2)
-            dst = rows.at[0, q, zl, z // 2, low, :, :, :, cols]
+            dst = rows.at[0, q, cl, ch, low, :, :, :, cols]
         elif kind == 1:
-            other = lax.rem(odd + xl + low, 2)
-            dst = rows.at[0, q, low, :, other, :, x // 2, :, cols]
+            dst = rows.at[0, q, low, :, other, :, ch, :, cols]
         else:
-            other = lax.rem(odd + yl + low, 2)
-            dst = rows.at[0, q, low, :, yl, y // 2, :, :, cols]
+            dst = rows.at[0, q, low, :, cl, ch, :, :, cols]
         return rb[kind].at[which, half, :, low, :, other], dst
 
     def sends(kind, which):
@@ -230,22 +228,35 @@
                     drain(pk[kind].at[half, pl.ds(0, 2)], r2.at[kind, half, which])
                     drain(rb[kind].at[0, 0, 0, 0], c2.at[kind, half, which])
                 away, to = sends(kind, which)
-
-                @pl.when(away)
+                far = order.c == mod4(to + 2)
+
+                def pace(low):
+                    if q:
+                        @pl.when(jnp.logical_not(is_root))
+                        def _():
+                            drain(rb[kind].at[0, 0, 0, 0], s3.at[kind, which, q - 1, low])
+
+                @pl.when(away & jnp.logical_not(far))
                 def _():
                     for low in range(2):
-                        if q:
-                            @pl.when(jnp.logical_not(is_root))
-                            def _():
-                                drain(rb[kind].at[0, 0, 0, 0], s3.at[kind, which, q - 1, low])
-
-                        src, dst = piece(kind, which, q, low)
+                        pace(low)
+                        src, dst = piece(kind, which, q, low, order.c)
                         remote(src, dst, s3.at[kind, which, q, low], r3.at[kind, q], order.at(a, b, to)).start()
 
+                @pl.when(far)
+                def _():
+                    for low in range(2):
+                        pace(low)
+                        src, _ = piece(kind, which, q, low, order.c)
+                        remote(
+                            src, rl[kind].at[which, q], s3.at[kind, which, q, low], r4.at[kind, which, q],
+                            order.at(a, b, mod4(order.c + 1 + 2 * low)),
+                        ).start()
+
                 @pl.when(jnp.logical_not(away))
                 def _():
                     for low in range(2):
-                        src, dst = piece(kind, which, q, low)
+                        src, dst = piece(kind, which, q, low, order.c)
                         pltpu.make_async_copy(src, dst, c3.at[kind, q]).start()
 
             pass_on(0)
@@ -253,6 +264,27 @@
             @pl.when(order.has_second(a, b))
             def _():
                 pass_on(1)
+
+    def beside(kind, which):
+        away, to = sends(kind, which)
+        near = away & (orders[kind].c != mod4(to + 2))
+        if which:
+            near = near & orders[kind].has_second(orders[kind].a, orders[kind].b)
+        return near, to
+
+    def relay(q):
+        for kind, order in enumerate(orders):
+            for which in range(2):
+                near, to = beside(kind, which)
+
+                @pl.when(near)
+                def _():
+                    drain(rb[kind].at[0, 0, 0, 0], r4.at[kind, which, q])
+                    low = jnp.where(order.c == mod4(to + 3), 0, 1)
+                    _, dst = piece(kind, which, q, low, mod4(to + 2))
+                    remote(
+                        rl[kind].at[which, q], dst, s4.at[kind, which, q], r3.at[kind, q], order.at(order.a, order.b, to)
+                    ).start()
 
     eye = lax.broadcasted_iota(jnp.int32, (256, 256), 0) == lax.broadcasted_iota(jnp.int32, (256, 256), 1)
 
@@ -361,9 +393,13 @@
     second_phase(0)
     second_phase(1)
     third_phase(0)
+    relay(0)
     third_phase(1)
+    relay(1)
     third_phase(2)
+    relay(2)
     third_phase(3)
+    relay(3)
 
     @pl.when(is_root)
     def _():
@@ -426,6 +462,15 @@
                 @pl.when(order.has_second(a, mod4(b + step)))
                 def _():
                     drain(rb[kind].at[0, 0, 0, 0], s2.at[kind, half, 1])
+
+    for kind in range(3):
+        for which in range(2):
+            near, _ = beside(kind, which)
+
+            @pl.when(near)
+            def _():
+                for q in range(4):
+                    drain(rb[kind].at[0, 0, 0, 0], s4.at[kind, which, q])
 
     for kind, order in enumerate(orders):
         for which in range(2):
@@ -520,6 +565,7 @@
             + [vmem((2, 4, 6, 16, w), bf) for w in widths]
             + [vmem((2, 2, 2, 6, 16, w), bf) for w in widths]
             + [vmem((2, 2, 2, 2, 2, 2, 16, w), bf) for w in widths]
+            + [vmem((2, 4, 2, 2, 16, w), bf) for w in widths]
             + [
                 vmem((2, 4, 2, 2, 2, 2, 2, 16, width), bf),
                 vmem((4, 512, 128), f32),
@@ -532,7 +578,7 @@
                 vmem((6, 16, 128), f32),
                 dma, dma, dma, dma((3, 2)), dma((3, 2)), dma((3, 2)),
                 dma((3, 2, 2)), dma((3, 2, 2)), dma((3, 2, 2)),
-                dma((3, 2, 4, 2)), dma((3, 4)), dma((3, 4)),
+                dma((3, 2, 4, 2)), dma((3, 4)), dma((3, 4)), dma((3, 2, 4)), dma((3, 2, 4)),
                 dma((3, 4)), dma((3, 4)), dma((4,)), dma((4,)), dma, dma, dma,
             ],
             compiler_params=pltpu.CompilerParams(

time: 60 us -> 56.3 us (0.938)
  Pallas kernels: 57.9 us -> 54.3 us
    pallas_call x1, Pallas kernels: 57.9 us -> 54.3 us  [step(): pl.pallas_call(kernel, out_shape=jax.ShapeDtypeStruct((2, 3, 1, 256), f32...]
where the time goes in v4:
time: 56.3 us; the launch traced here: 56.2 us
  Pallas kernels  54.3 us (96%)
  local copies, waits for them, and re-layouts  1.26 us (2%)
  between operations  0.64 us (1%)
    pallas_call x1, Pallas kernels, step(): pl.pallas_call(kernel, out_shape=jax.ShapeDtypeStruct((2, 3, 1, 256), f32...  54.3 us
    unnamed x1, local copies, waits for them, and re-layouts  1.26 us

profile of v4, /device:TPU:1, one launch (start us, length us, event | category | flops | bytes accessed | tf_op | source)
XLA Modules:
  0.0 56.2 jit_solution(3182419426827671892)
XLA Ops:
  0.6 54.3 %shard_map.50 = f32[2,3,1,256]{3,2,1,0:T(1,128)} custom-call(bf16[384,1024]{1,0:T(8,128)(2,1)} %embeds.1, s32[384]{0:T(512)} %cluster_id.1, s32[24]{0:T(128)} %owner_slot.1), custom_call_target="tpu_custom_call" | custom-call | tf_op jit(solution)/shard_map/pallas_call | solution.py:559
  54.9 1.3 %slice_bitcast_fusion = (f32[1,1,3,256]{3,1,2,0:T(1,128)}, f32[1,1,3,256]{3,1,2,0:T(1,128)}) fusion(f32[2,3,1,256]{3,2,1,0:T(1,128)} %shard_map.50), kind=kLoop, calls=%fused_computation | loop fusion | bytes 12288

commit v5 on v4

--- a/solution.py
+++ b/solution.py
@@ -22,11 +22,11 @@
 def place():
     g = lax.axis_index("group")
     d = lax.axis_index("dev")
-    return mod4(lax.rem(d, 4) + 0), mod4(g // 2 + 0), mod4(d // 4 + 1), lax.rem(g, 2)
+    return mod4(lax.rem(d, 4) + 3), mod4(g // 2 + 0), mod4(d // 4 + 1), lax.rem(g, 2)
 
 
 def device(x, y, z, core):
-    return (mod4(y - 0) * 2 + core, mod4(z - 1) * 4 + mod4(x - 0))
+    return (mod4(y - 0) * 2 + core, mod4(z - 1) * 4 + mod4(x - 3))
 
 
 def root_of(g, l):
@@ -434,24 +434,20 @@
                         stats[part, lane, line : line + 1] = value[:, lane * 128 : lane * 128 + 128]
         spot = root_l * 2 + core
         for step in range(16):
-            row = mod4(z + step // 4)
-            column = mod4(x + step % 4)
+            row, column = (1 + step // 4) % 4, (3 + step) % 4
             target = device(column, y, row, lax.rem(root_g, 2))
-            src = stats.at[lax.rem(row, 2), row // 2]
-            if step:
+            src = stats.at[row % 2, row // 2]
+            same = (x == column) & (z == row) & (core == lax.rem(root_g, 2))
+
+            @pl.when(jnp.logical_not(same))
+            def _():
                 remote(src, landed.at[spot], so, ro, target).start()
-            else:
-                same = core == lax.rem(root_g, 2)
-
-                @pl.when(jnp.logical_not(same))
-                def _():
-                    remote(src, landed.at[spot], so, ro, target).start()
-
-                @pl.when(same)
-                def _():
-                    copy = pltpu.make_async_copy(src, landed.at[spot], co)
-                    copy.start()
-                    copy.wait()
+
+            @pl.when(same)
+            def _():
+                copy = pltpu.make_async_copy(src, landed.at[spot], co)
+                copy.start()
+                copy.wait()
 
     for half in range(HALVES):
         for kind, order in enumerate(orders):

time: 56.3 us -> 55.8 us (level)
  Pallas kernels: 54.3 us -> 53.7 us
    pallas_call x1, Pallas kernels: 54.3 us -> 53.7 us  [step(): pl.pallas_call(kernel, out_shape=jax.ShapeDtypeStruct((2, 3, 1, 256), f32...]
where the time goes in v5:
time: 55.8 us; the launch traced here: 55.6 us
  Pallas kernels  53.7 us (96%)
  local copies, waits for them, and re-layouts  1.26 us (2%)
  between operations  0.64 us (1%)
    pallas_call x1, Pallas kernels, step(): pl.pallas_call(kernel, out_shape=jax.ShapeDtypeStruct((2, 3, 1, 256), f32...  53.7 us
    unnamed x1, local copies, waits for them, and re-layouts  1.26 us

profile of v5, /device:TPU:1, one launch (start us, length us, event | category | flops | bytes accessed | tf_op | source)
XLA Modules:
  0.0 55.6 jit_solution(13119597948900128707)
XLA Ops:
  0.6 53.7 %shard_map.50 = f32[2,3,1,256]{3,2,1,0:T(1,128)} custom-call(bf16[384,1024]{1,0:T(8,128)(2,1)} %embeds.1, s32[384]{0:T(512)} %cluster_id.1, s32[24]{0:T(128)} %owner_slot.1), custom_call_target="tpu_custom_call" | custom-call | tf_op jit(solution)/shard_map/pallas_call | solution.py:555
  54.3 1.3 %slice_bitcast_fusion = (f32[1,1,3,256]{3,1,2,0:T(1,128)}, f32[1,1,3,256]{3,1,2,0:T(1,128)}) fusion(f32[2,3,1,256]{3,2,1,0:T(1,128)} %shard_map.50), kind=kLoop, calls=%fused_computation | loop fusion | bytes 12288

commit v6 on v5

--- a/solution.py
+++ b/solution.py
@@ -11,7 +11,7 @@
 MESH = pl.DeviceIdType.MESH
 SHARP = 20.0 * math.log2(math.e)
 ABSENT = -1e30
-COLS = ((0, 384), (384, 768), (768, 1024))
+COLS = ((0, 256), (256, 640), (640, 1024))
 HALVES = 2
 
 

time: 55.8 us -> 54.7 us (0.980)
  Pallas kernels: 53.7 us -> 52.5 us
    pallas_call x1, Pallas kernels: 53.7 us -> 52.5 us  [step(): pl.pallas_call(kernel, out_shape=jax.ShapeDtypeStruct((2, 3, 1, 256), f32...]
where the time goes in v6:
time: 54.7 us; the launch traced here: 54.4 us
  Pallas kernels  52.5 us (96%)
  local copies, waits for them, and re-layouts  1.26 us (2%)
  between operations  0.64 us (1%)
    pallas_call x1, Pallas kernels, step(): pl.pallas_call(kernel, out_shape=jax.ShapeDtypeStruct((2, 3, 1, 256), f32...  52.5 us
    unnamed x1, local copies, waits for them, and re-layouts  1.26 us

profile of v6, /device:TPU:1, one launch (start us, length us, event | category | flops | bytes accessed | tf_op | source)
XLA Modules:
  0.0 54.4 jit_solution(13840746823199577348)
XLA Ops:
  0.6 52.5 %shard_map.50 = f32[2,3,1,256]{3,2,1,0:T(1,128)} custom-call(bf16[384,1024]{1,0:T(8,128)(2,1)} %embeds.1, s32[384]{0:T(512)} %cluster_id.1, s32[24]{0:T(128)} %owner_slot.1), custom_call_target="tpu_custom_call" | custom-call | tf_op jit(solution)/shard_map/pallas_call | solution.py:555
  53.1 1.3 %slice_bitcast_fusion = (f32[1,1,3,256]{3,1,2,0:T(1,128)}, f32[1,1,3,256]{3,1,2,0:T(1,128)}) fusion(f32[2,3,1,256]{3,2,1,0:T(1,128)} %shard_map.50), kind=kLoop, calls=%fused_computation | loop fusion | bytes 12288
